TPU v7x, 256 devices: a whole 4x4x8 slice. The times are simulated.
256 devices in a mesh: blk: 128 (over x, y, z), ch: 2 (over core).
Axes of the slice: x: 4, y: 4, z: 8, core: 2. Of those that a mesh axis runs over, the one named last changes fastest.
Arguments:
- blocks: float32 [8, 128, 256, 256], P(None, 'blk', None, 'ch'), may hold values from -1 to 5, as said below
Outputs:
- factor: float32 [4, 8, 128, 256, 256], P(None, None, 'blk', None, 'ch')
- second_row: float32 [8, 128, 256, 256], P(None, 'blk', None, 'ch')
Inputs may be any that keep to these rules, and one draw needn't show every extreme that they name: blocks[0, 0] is symmetric, and the block-Toeplitz matrix built from the first 5 block columns is positive definite.
All inputs are finite; a program needn't handle non-finite values. Where the computation divides by a largest or mean magnitude, that divisor is 1e-20 or more.
Results may differ from a plain program's by a relative error of at most 0.0003.
Values sent between devices are 32-bit elements; how exact they have to be, the bound alone decides.
A program may use at most 64 MiB of HBM per device.

v0:
```python
import jax
import jax.numpy as jnp
from jax import lax
from jax.sharding import PartitionSpec as P

STEPS = 3


def passed_along(array, axis, by):
    peers = lax.axis_size(axis)
    return lax.ppermute(array, axis, [(i, (i + by) % peers) for i in range(peers)])


def broadcast(block, axis, owner):
    block = jnp.where(lax.axis_index(axis) == owner, block, jnp.zeros_like(block))
    return lax.psum(block, axis)


def matmul(left, right):
    return jnp.dot(left, right, precision=lax.Precision.HIGHEST)


def root_inverse(matrix, sweeps):
    identity = jnp.eye(matrix.shape[0], dtype=matrix.dtype)
    scaling = jnp.max(jnp.sum(jnp.abs(matrix), axis=1))
    approach = matrix / scaling
    inv_part = identity
    for sweep_index in range(sweeps):
        middle = 1.5 * identity - 0.5 * matmul(inv_part, approach)
        approach = matmul(approach, middle)
        inv_part = matmul(middle, inv_part)
    return inv_part / jnp.sqrt(scaling)


def inverse_newton(matrix, sweeps):
    identity = jnp.eye(matrix.shape[0], dtype=matrix.dtype)
    scaling = jnp.max(jnp.sum(jnp.abs(matrix), axis=1))
    guess = identity / scaling
    for sweep_index in range(sweeps):
        guess = matmul(guess, 2.0 * identity - matmul(matrix, guess))
    return guess


def make_rotation(lead_upper, lead_second):
    width = lead_upper.shape[0]
    identity = jnp.eye(width, dtype=lead_upper.dtype)
    gram = matmul(lead_upper, lead_upper.T)
    cross = matmul(lead_upper, lead_second.T)
    coupling_t = matmul(inverse_newton(gram, 5), cross)
    coupling = coupling_t.T
    first_inv = root_inverse(identity - matmul(coupling_t, coupling), 5)
    second_inv = root_inverse(identity - matmul(coupling, coupling_t), 5)
    top_rows = jnp.concatenate([first_inv, -matmul(first_inv, coupling_t)], axis=1)
    bottom_rows = jnp.concatenate([-matmul(second_inv, coupling), second_inv], axis=1)
    return jnp.concatenate([top_rows, bottom_rows], axis=0)


def pass_on(row_blocks):
    arrived = passed_along(row_blocks, "blk", -1)
    rolled = jnp.concatenate([arrived[1:], jnp.zeros_like(arrived[:1])], axis=0)
    is_final = lax.axis_index("blk") == lax.axis_size("blk") - 1
    return jnp.where(is_final, rolled, arrived)


def body(blocks):
    local = blocks[:, 0]
    width = local.shape[1]
    first_half = broadcast(local[0], "blk", 0)
    first_whole = lax.all_gather(first_half, "ch", axis=1, tiled=True)
    first_inv = root_inverse(first_whole, 6)
    upper_row = jnp.einsum("ab,jbc->jac", first_inv, local, precision=lax.Precision.HIGHEST)
    lower_row = pass_on(upper_row)
    collected = [upper_row]
    for step_index in range(STEPS):
        pair_half = jnp.stack([upper_row[0], lower_row[0]])
        pair_whole = lax.all_gather(pair_half, "ch", axis=2, tiled=True)
        rotation = make_rotation(pair_whole[0], pair_whole[1])
        rotation = broadcast(rotation, "blk", 0)
        joined = jnp.concatenate([upper_row, lower_row], axis=1)
        moved = jnp.einsum("ab,jbc->jac", rotation, joined, precision=lax.Precision.HIGHEST)
        upper_row = moved[:, :width]
        lower_row = moved[:, width:]
        collected.append(upper_row)
        lower_row = pass_on(lower_row)
    factor = jnp.stack(collected)[:, :, None]
    return (factor, lower_row[:, None])


def solution(mesh):
    placed = (P(None, "blk", None, "ch"),)
    return jax.shard_map(
        body,
        mesh=mesh,
        in_specs=placed,
        out_specs=(P(None, None, "blk", None, "ch"), P(None, "blk", None, "ch")),
        check_vma=False,
    )
```

profile of v0, /device:TPU:1, one launch (start us, length us, event | category | flops | bytes accessed | tf_op | source)
XLA Modules:
  0.0 1130.5 jit_solution(199383222002910405)
XLA Ops:
  7.2 1.6 select_bitcast_fusion.1
  8.9 216.1 %all-reduce.9.cloned.1.call-done = f32[256,128]{1,0:T(8,128)} async-done(((f32[256,128]{1,0:T(8,128)}), f32[256,128]{1,0:T(8,128)}) %all-reduce.9.cloned.1.call-update) | async-done | bytes 131088 | tf_op jit(solution)/shard_map/psum | solution.py:16
  224.9 6.9 all_gather.12
  232.6 1.0 select_subtract_fusion.35
  233.5 1.0 fusion.61
  241.0 1.0 fusion.25
  242.1 4.6 collective-permute-start
  246.7 22.2 %collective-permute-done = f32[8,256,128]{2,1,0:T(8,128)S(1)} collective-permute-done((f32[8,256,128]{2,1,0:T(8,128)S(1)}, f32[8,256,128]{2,1,0:T(8,128)S(1)}, u32[]{:S(2)}, u32[]{:S(2)}) %collective-permute-start) | collective-permute-done | bytes 1048608 | tf_op jit(solution)/shard_map/ppermute | solution.py:11
  269.1 3.4 all_gather.13
  281.1 1.0 select_subtract_fusion.29
  282.1 1.0 fusion.62
  288.9 1.0 select_subtract_fusion.24
  289.8 1.0 fusion.63
  298.5 1.1 maximum_select_fusion
  299.7 214.8 %all-reduce.11.cloned.1.call-done = f32[512,512]{0,1:T(8,128)} async-done(((f32[512,512]{0,1:T(8,128)}), f32[512,512]{0,1:T(8,128)}) %all-reduce.11.cloned.1.call-update) | async-done | bytes 1048592 | tf_op jit(solution)/shard_map/psum | solution.py:16
  514.5 4.8 fusion.18
  519.3 1.2 slice_bitcast_fusion.17
  520.6 5.2 collective-permute-start.1
  525.8 17.9 %collective-permute-done.1 = f32[8,256,128]{2,1,0:T(8,128)S(1)} collective-permute-done((f32[8,256,128]{2,1,0:T(8,128)S(1)}, f32[8,256,128]{2,1,0:T(8,128)S(1)}, u32[]{:S(2)}, u32[]{:S(2)}) %collective-permute-start.1) | collective-permute-done | bytes 1048608 | tf_op jit(solution)/shard_map/ppermute | solution.py:11
  543.9 7.5 all_gather.14
  551.8 1.1 fusion.37
  559.7 1.1 abs_reduce_fusion.4
  560.8 0.7 reduce_max.95
  561.5 2.0 select_subtract_fusion.19
  563.5 2.0 fusion.64
  568.5 1.1 fusion.113
  569.6 1.1 fusion.112
  571.4 1.3 abs_reduce_fusion.3
  573.4 1.9 select_subtract_fusion.14
  575.3 2.0 fusion.65
  577.2 0.7 fusion.41
  580.6 1.1 fusion.119
  581.7 1.1 fusion.118
  583.5 1.5 select_subtract_fusion.15
  585.0 1.5 convolution_divide_fusion.3
  588.6 1.1 maximum_select_fusion.1
  589.7 214.8 %all-reduce.13.cloned.1.call-done = f32[512,512]{0,1:T(8,128)} async-done(((f32[512,512]{0,1:T(8,128)}), f32[512,512]{0,1:T(8,128)}) %all-reduce.13.cloned.1.call-update) | async-done | bytes 1048592 | tf_op jit(solution)/shard_map/psum | solution.py:16
  804.5 4.8 fusion.15
  809.3 1.2 slice_bitcast_fusion.16
  810.6 5.2 collective-permute-start.2
  815.8 17.8 %collective-permute-done.2 = f32[8,256,128]{2,1,0:T(8,128)S(1)} collective-permute-done((f32[8,256,128]{2,1,0:T(8,128)S(1)}, f32[8,256,128]{2,1,0:T(8,128)S(1)}, u32[]{:S(2)}, u32[]{:S(2)}) %collective-permute-start.2) | collective-permute-done | bytes 1048608 | tf_op jit(solution)/shard_map/ppermute | solution.py:11
  833.8 7.5 all_gather.15
  841.8 1.1 fusion.36
  849.6 1.1 abs_reduce_fusion.1
  850.7 0.7 reduce_max.98
  851.4 2.0 select_subtract_fusion.9
  853.3 2.0 fusion.66
  858.3 1.1 fusion.130
  859.4 1.1 fusion.129
  861.2 1.3 abs_reduce_fusion
  862.5 0.7 reduce_max.99
  863.2 2.0 select_subtract_fusion.4
  865.2 2.0 fusion.67
  870.4 1.1 fusion.136
  871.5 1.1 fusion.135
  873.3 1.5 select_subtract_fusion.5
  874.8 1.5 convolution_divide_fusion.1
  878.4 1.2 maximum_select_fusion.2
  879.6 214.9 %all-reduce.15.cloned.1.call-done = f32[512,512]{0,1:T(8,128)} async-done(((f32[512,512]{0,1:T(8,128)}), f32[512,512]{0,1:T(8,128)}) %all-reduce.15.cloned.1.call-update) | async-done | bytes 1048592 | tf_op jit(solution)/shard_map/psum | solution.py:16
  1094.5 4.8 fusion.12
  1099.5 5.3 collective-permute-start.3
  1104.7 2.3 maximum_bitcast_fusion
  1107.1 15.5 %collective-permute-done.3 = f32[8,256,128]{2,1,0:T(8,128)S(1)} collective-permute-done((f32[8,256,128]{2,1,0:T(8,128)S(1)}, f32[8,256,128]{2,1,0:T(8,128)S(1)}, u32[]{:S(2)}, u32[]{:S(2)}) %collective-permute-start.3) | collective-permute-done | bytes 1048608 | tf_op jit(solution)/shard_map/ppermute | solution.py:11
  1122.7 1.1 select_bitcast_fusion
  (170 shorter events, 56.1 us)
Async XLA Ops:
  7.2 217.8 %all-reduce.9.cloned.1.call-start = ((), (), s32[]{:S(2)}) async-start(), calls=%async_computation | async-start | bytes 262144 | tf_op jit(solution)/shard_map/psum | solution.py:16
  8.8 505.7 %all-reduce.11.cloned.1.call-start = ((), (), s32[]{:S(2)}) async-start(), calls=%async_computation.1 | async-start | bytes 2097152 | tf_op jit(solution)/shard_map/psum | solution.py:16
  238.4 2.6 copy-start.2
  242.1 26.8 %collective-permute-start = (f32[8,256,128]{2,1,0:T(8,128)S(1)}, f32[8,256,128]{2,1,0:T(8,128)S(1)}, u32[]{:S(2)}, u32[]{:S(2)}) collective-permute-start(f32[8,256,128]{2,1,0:T(8,128)S(1)} %bitcast.325), channel_id=1, source_target_pairs={{0,254},{2,0},{4,2},{6,4},{8,6},{10,8},{12,10},{14,12},{16,14},{18... | collective-permute-start | bytes 3145736 | tf_op jit(solution)/shard_map/ppermute | solution.py:11
  299.6 504.9 %all-reduce.13.cloned.1.call-start = ((), (), s32[]{:S(2)}) async-start(), calls=%async_computation.2 | async-start | bytes 2097152 | tf_op jit(solution)/shard_map/psum | solution.py:16
  520.6 23.1 %collective-permute-start.1 = (f32[8,256,128]{2,1,0:T(8,128)S(1)}, f32[8,256,128]{2,1,0:T(8,128)S(1)}, u32[]{:S(2)}, u32[]{:S(2)}) collective-permute-start(f32[8,256,128]{2,1,0:T(8,128)S(1)} %get-tuple-element.7), channel_id=1, source_target_pairs={{0,254},{2,0},{4,2},{6,4},{8,6},{10,8},{12,10},{14,12},{16,14},{18... | collective-permute-start | bytes 3145736 | tf_op jit(solution)/shard_map/ppermute | solution.py:11
  556.9 2.4 copy-start.4
  583.5 3.7 copy-start.5
  583.5 3.7 copy-start.6
  589.7 504.8 %all-reduce.15.cloned.1.call-start = ((), (), s32[]{:S(2)}) async-start(), calls=%async_computation.3 | async-start | bytes 2097152 | tf_op jit(solution)/shard_map/psum | solution.py:16
  810.6 23.1 %collective-permute-start.2 = (f32[8,256,128]{2,1,0:T(8,128)S(1)}, f32[8,256,128]{2,1,0:T(8,128)S(1)}, u32[]{:S(2)}, u32[]{:S(2)}) collective-permute-start(f32[8,256,128]{2,1,0:T(8,128)S(1)} %get-tuple-element.10), channel_id=1, source_target_pairs={{0,254},{2,0},{4,2},{6,4},{8,6},{10,8},{12,10},{14,12},{16,14},{18... | collective-permute-start | bytes 3145736 | tf_op jit(solution)/shard_map/ppermute | solution.py:11
  846.8 2.4 copy-start.3
  873.3 3.7 copy-start.7
  873.3 3.7 copy-start.8
  1099.2 5.5 copy-start
  1099.3 5.5 copy-start.1
  1099.5 23.1 %collective-permute-start.3 = (f32[8,256,128]{2,1,0:T(8,128)S(1)}, f32[8,256,128]{2,1,0:T(8,128)S(1)}, u32[]{:S(2)}, u32[]{:S(2)}) collective-permute-start(f32[8,256,128]{2,1,0:T(8,128)S(1)} %get-tuple-element.4), channel_id=1, source_target_pairs={{0,254},{2,0},{4,2},{6,4},{8,6},{10,8},{12,10},{14,12},{16,14},{18... | collective-permute-start | bytes 3145736 | tf_op jit(solution)/shard_map/ppermute | solution.py:11
Sparse Core Ops, SparseCore 0:
  14.0 210.8 all-reduce.8
  299.8 214.7 all-reduce.10
  589.8 214.6 all-reduce.12
  879.7 214.7 all-reduce.14
where the time goes:
time: 1140 us; the launch traced here: 1130 us
  waiting for transfers between devices  934 us (82%)
  matrix products  110 us (10%)
  blocking collectives  25.4 us (2%)
  between operations  22.4 us (2%)
  starting transfers between devices  20.4 us (2%)
  other arithmetic  15.4 us (1%)
    psum x4, waiting for transfers between devices, broadcast(): return lax.psum(block, axis)  861 us
    dot_general x152, matrix products, matmul(): return jnp.dot(left, right, precision=lax.Precision.HIGHEST)  94.5 us
    ppermute x4, waiting for transfers between devices, passed_along(): lax.ppermute(array, axis, [(i, (i + by) % peers) for i in range(peers)])  73.4 us
  transfers between devices with their start and end apart: 8, of which 8 were waited for; matrix products, arithmetic and copies ran while one was open for 0% of the time, Pallas kernels for 0%

commit v1 on v0

v1 whole, which is shorter than its diff:
```python
import functools

import jax
import jax.numpy as jnp
from jax import lax
from jax.experimental import pallas as pl
from jax.experimental.pallas import tpu as pltpu
from jax.sharding import PartitionSpec as P

MESH = pl.DeviceIdType.MESH
F32, BF16 = jnp.float32, jnp.bfloat16

STEPS = 3
LEADS = STEPS + 1
REACH = STEPS + 1
DEPTH = 8
DOWN = 5
FAR = 5


def split(a):
    high = a.astype(BF16)
    return high, (a - high.astype(F32)).astype(BF16)


def dot_of_parts(left, right):
    (lh, ll), (rh, rl) = left, right
    return jnp.dot(
        jnp.concatenate([lh, ll, lh], axis=1),
        jnp.concatenate([rh, rh, rl], axis=0),
        preferred_element_type=F32,
    )


def mul(left, right):
    return dot_of_parts(split(left), split(right))


def wait_for(ref, sem):
    pltpu.make_async_copy(ref, ref, sem).wait()


def kernel(n, depth, x_ref, factor_ref, second_ref, halo, lead, why, zed, stage, coef_high, coef_low, a_ref, c_ref,
           scatter_send, z_send, piece_recv, plane_send, plane_recv, sib_send, sib_recv,
           down_send, down_recv, up_send, up_recv, out_sem):
    width = x_ref.shape[1]
    count = x_ref.shape[0]
    half = x_ref.shape[2]
    ups = count - DOWN
    b, ch = lax.axis_index("blk"), lax.axis_index("ch")
    planes = n // depth
    rows = width // planes
    p, z = lax.div(b, depth), lax.rem(b, depth)
    below, above, far_below = lax.rem(b + n - 1, n), lax.rem(b + 1, n), lax.rem(b + n - FAR, n)

    def in_plane(i):
        return {"blk": lax.rem(p + i, planes) * depth + z}

    def in_line(i):
        return {"blk": p * depth + lax.rem(z + i, depth)}

    sibling = {"ch": 1 - ch}

    def each(start, stop, body):
        def run(i, carry):
            body(i)
            return carry

        lax.fori_loop(start, stop, run, 0)

    def push(src, dst, send, recv, to):
        return pltpu.make_async_remote_copy(
            src_ref=src, dst_ref=dst, send_sem=send, recv_sem=recv, device_id=to, device_id_type=MESH
        )

    barrier = pltpu.get_barrier_semaphore()

    def greet(to):
        pl.semaphore_signal(barrier, inc=1, device_id=to, device_id_type=MESH)

    for by in (1, n - 1, FAR, n - FAR):
        greet({"blk": lax.rem(b + by, n)})
    greet(sibling)
    each(1, planes, lambda i: greet(in_plane(i)))
    each(1, depth, lambda i: greet(in_line(i)))
    pl.semaphore_wait(barrier, 4 + 1 + (planes - 1) + (depth - 1))

    def piece(item, i):
        return lead.at[item, ch, pl.ds(pl.multiple_of(i * rows, rows), rows)]

    def own_piece(i):
        return x_ref.at[0, pl.ds(pl.multiple_of(i * rows, rows), rows)]

    def scatter_copy(i):
        return push(own_piece(i), piece(b, i), scatter_send.at[i], piece_recv.at[b], {"blk": i * depth + b})

    def line_copy(item, i):
        return push(piece(item, p), piece(item, p), z_send.at[i], piece_recv.at[item], in_line(i))

    def plane_copy(item, i):
        return push(piece(item, p), piece(item, p), plane_send.at[item, i], plane_recv.at[item], in_plane(i))

    def sibling_copy(item):
        return push(lead.at[item, ch], lead.at[item, ch], sib_send.at[item], sib_recv.at[item], sibling)

    @pl.when(b < LEADS)
    def _():
        pltpu.make_async_copy(own_piece(0), piece(b, 0), piece_recv.at[b]).start()
        each(1, planes, lambda i: scatter_copy(i).start())

    def down_copy(t, src):
        s, r = lax.div(t, DOWN), lax.rem(t, DOWN)
        return push(src, halo.at[s, r], down_send.at[t], down_recv.at[t], {"blk": below})

    def up_copy(t, src, to):
        s, r = FAR - 1 - lax.div(t, ups), DOWN + lax.rem(t, ups)
        return push(src, halo.at[s, r], up_send.at[t], up_recv.at[t], {"blk": to})

    def down_source(t):
        return halo.at[lax.div(t, DOWN) - 1, lax.rem(t, DOWN)]

    def up_source(t):
        return halo.at[FAR - lax.div(t, ups), DOWN + lax.rem(t, ups)]

    n_down, n_up = REACH * DOWN, (REACH + 1) * ups

    def down_arrived(t):
        wait_for(halo.at[lax.div(t, DOWN), lax.rem(t, DOWN)], down_recv.at[t])

    def up_arrived(t):
        wait_for(halo.at[FAR - 1 - lax.div(t, ups), DOWN + lax.rem(t, ups)], up_recv.at[t])

    def relay(t):
        @pl.when(t < n_down - DOWN)
        def _():
            down_arrived(t)
            down_copy(t + DOWN, down_source(t + DOWN)).start()

        @pl.when(t < n_up - ups)
        def _():
            up_arrived(t)
            up_copy(t + ups, up_source(t + ups), above).start()

    each(0, ups, lambda t: up_copy(t, x_ref.at[DOWN + t], far_below).start())
    each(0, 1, lambda t: down_copy(t, x_ref.at[t]).start())

    def pass_piece(item):
        wait_for(piece(item, p), piece_recv.at[item])

        @pl.when(z == item)
        def _():
            each(1, depth, lambda i: line_copy(item, i).start())

        each(1, planes, lambda i: plane_copy(item, i).start())

    each(0, LEADS, pass_piece)
    each(1, DOWN, lambda t: down_copy(t, x_ref.at[t]).start())

    def gathered(item):
        if planes > 1:
            wait_for(lead.at[item, ch, pl.ds(0, (planes - 1) * rows)], plane_recv.at[item])
        sibling_copy(item).start()

    def complete(item):
        wait_for(lead.at[item, 1 - ch], sib_recv.at[item])

    def lead_block(item):
        return jnp.concatenate([lead[item, 0], lead[item, 1]], axis=1)

    eye = (
        lax.broadcasted_iota(jnp.int32, (width, width), 0) == lax.broadcasted_iota(jnp.int32, (width, width), 1)
    ).astype(F32)

    def scale_of(a):
        return jnp.max(jnp.sum(jnp.abs(a), axis=0, keepdims=True), axis=1, keepdims=True)

    def roots(matrices, sweeps, first_tick):
        kept = range(len(matrices))
        scales = [scale_of(a) for a in matrices]
        starts = [a * (1.0 / s) for a, s in zip(matrices, scales)]
        middles = [1.5 * eye - 0.5 * y for y in starts]
        firsts = [mul(y, t) for y, t in zip(starts, middles)]
        for i in kept:
            zed[i] = middles[i]
            why[i] = firsts[i]

        def sweep(k, carry):
            relay(first_tick + k)
            ys = [split(why[i]) for i in kept]
            zs = [split(zed[i]) for i in kept]
            ts = [split(1.5 * eye - 0.5 * dot_of_parts(zs[i], ys[i])) for i in kept]
            new_ys = [dot_of_parts(ys[i], ts[i]) for i in kept]
            new_zs = [dot_of_parts(ts[i], zs[i]) for i in kept]
            for i in kept:
                why[i] = new_ys[i]
                zed[i] = new_zs[i]
            return carry

        lax.fori_loop(0, sweeps - 1, sweep, 0)
        return scales

    def cols(j, k=1):
        return pl.ds(j * width, k * width)

    def keep_coefficients(o, value, terms):
        high, low = split(value)
        coef_high[o, :, : terms * width] = high
        coef_low[o, :, : terms * width] = low

    gathered(0)
    complete(0)
    (s,) = roots([lead_block(0)], 6, 0)
    root = jnp.sqrt(s)
    w = zed[0] * (1.0 / root)
    x0 = why[0] * root
    for item in range(1, LEADS):
        gathered(item)
    for item in range(1, LEADS):
        complete(item)
    rest = mul(w, jnp.concatenate([lead_block(item) for item in range(1, LEADS)], axis=1))
    uppers = [x0] + [rest[:, i * width : (i + 1) * width] for i in range(LEADS - 1)]
    lowers = uppers[1:]
    keep_coefficients(0, w, 1)
    a_ref[:, cols(0)] = w
    c_ref[:, cols(0)] = w
    tick = 5

    for k in range(STEPS):
        terms = k + 1
        x, y = uppers[0], lowers[0]
        both = mul(x, jnp.concatenate([x.T, y.T], axis=1))
        gram, cross = both[:, :width], both[:, width:]
        s = 1.0 / scale_of(gram)
        power = eye - gram * s
        total = cross * s
        for i in range(4):
            both = mul(power, jnp.concatenate([power, total], axis=1))
            power, total = both[:, :width], total + both[:, width:]
        kt = total + mul(power, total)
        kk = kt.T
        kt_parts, kk_parts = split(kt), split(kk)
        scales = roots([eye - dot_of_parts(kt_parts, kk_parts), eye - dot_of_parts(kk_parts, kt_parts)], 5, tick)
        tick += 4
        first = zed[0] * (1.0 / jnp.sqrt(scales[0]))
        second = zed[1] * (1.0 / jnp.sqrt(scales[1]))
        first_parts, second_parts = split(first), split(second)
        more = STEPS - 1 - k
        if more > 0:
            d = jnp.concatenate(uppers[:more], axis=1) - dot_of_parts(
                kt_parts, split(jnp.concatenate(lowers[:more], axis=1)))
            e = jnp.concatenate(lowers[1 : more + 1], axis=1) - dot_of_parts(
                kk_parts, split(jnp.concatenate(uppers[1 : more + 1], axis=1)))
            d = dot_of_parts(first_parts, split(d))
            e = dot_of_parts(second_parts, split(e))
            uppers = [d[:, i * width : (i + 1) * width] for i in range(more)]
            lowers = [e[:, i * width : (i + 1) * width] for i in range(more)]
        a, c = a_ref[:, cols(0, terms)], c_ref[:, cols(0, terms)]
        ktc = dot_of_parts(kt_parts, split(c))
        kka = dot_of_parts(kk_parts, split(a))
        none = jnp.zeros((width, width), F32)
        d = jnp.concatenate([a, none], axis=1) - jnp.concatenate([none, ktc], axis=1)
        e = jnp.concatenate([none, c], axis=1) - jnp.concatenate([kka, none], axis=1)
        a = dot_of_parts(first_parts, split(d))
        c = dot_of_parts(second_parts, split(e))
        a_ref[:, cols(0, terms + 1)] = a
        c_ref[:, cols(0, terms + 1)] = c
        keep_coefficients(k + 1, a, terms + 1)
        if k == STEPS - 1:
            keep_coefficients(STEPS + 1, c, terms + 1)

    def data(j, q):
        wrapped = (b + j >= n).astype(jnp.int32)
        blocks = []
        for i in range(2):
            r = 2 * q + i
            if j == 0:
                blocks.append(x_ref[r])
            else:
                block = halo[j - 1, jnp.minimum(r + wrapped, count - 1)]
                blocks.append(jnp.where(r + wrapped < count, block, jnp.zeros_like(block)))
        return split(jnp.concatenate(blocks, axis=1))

    def out_copy(o, q):
        target = factor_ref.at[o, pl.ds(2 * q, 2)] if o <= STEPS else second_ref.at[pl.ds(2 * q, 2)]
        return pltpu.make_async_copy(stage.at[o, pl.ds(2 * q, 2)], target, out_sem.at[o, q])

    def emit(o, q, parts):
        terms = len(parts)
        high, low = coef_high[o, :, : terms * width], coef_low[o, :, : terms * width]
        rh = jnp.concatenate([part[0] for part in parts], axis=0)
        rl = jnp.concatenate([part[1] for part in parts], axis=0)
        value = dot_of_parts((high, low), (rh, rl))
        stage[o, 2 * q] = value[:, :half]
        stage[o, 2 * q + 1] = value[:, half:]
        out_copy(o, q).start()

    def emit_pair(q, outputs):
        last = REACH if STEPS + 1 in outputs else max(outputs)
        parts = [data(j, q) for j in range(last + 1)]
        for o in outputs:
            emit(o, q, parts[: o + 1] if o <= STEPS else parts[1:])

    each(0, 4, lambda q: emit_pair(q, [0]))
    each(0, 2, lambda q: emit_pair(q, [1, 2, 3]))
    each(n_down - DOWN, n_down, down_arrived)
    each(0, 2, lambda q: emit_pair(q, [4]))
    each(n_up - ups, n_up, up_arrived)
    each(2, 4, lambda q: emit_pair(q, [1, 2, 3, 4]))

    @pl.when(b < LEADS)
    def _():
        each(1, planes, lambda i: scatter_copy(i).wait_send())
        each(1, depth, lambda i: line_copy(b, i).wait_send())

    @pl.when((b >= LEADS) & (z < LEADS))
    def _():
        each(1, depth, lambda i: line_copy(z, i).wait_send())

    for item in range(LEADS):
        each(1, planes, lambda i: plane_copy(item, i).wait_send())
        sibling_copy(item).wait_send()
    each(0, n_down, lambda t: down_copy(t, x_ref.at[0]).wait_send())
    each(0, n_up, lambda t: up_copy(t, x_ref.at[0], above).wait_send())
    for o in range(STEPS + 2):
        each(0, 4, lambda q: out_copy(o, q).wait())


def body(n, depth, blocks):
    local = blocks[:, 0]
    count, width, half = local.shape
    ups = count - DOWN
    planes = n // depth
    dma = pltpu.SemaphoreType.DMA
    any_space = pl.BlockSpec(memory_space=pl.ANY)
    factor, second = pl.pallas_call(
        functools.partial(kernel, n, depth),
        out_shape=(
            jax.ShapeDtypeStruct((STEPS + 1, count, width, half), F32),
            jax.ShapeDtypeStruct((count, width, half), F32),
        ),
        in_specs=[pl.BlockSpec(memory_space=pltpu.VMEM)],
        out_specs=(any_space, any_space),
        scratch_shapes=[
            pltpu.VMEM((FAR, count, width, half), F32),
            pltpu.VMEM((LEADS, 2, width, half), F32),
            pltpu.VMEM((2, width, width), F32),
            pltpu.VMEM((2, width, width), F32),
            pltpu.VMEM((STEPS + 2, count, width, half), F32),
            pltpu.VMEM((STEPS + 2, width, (STEPS + 1) * width), BF16),
            pltpu.VMEM((STEPS + 2, width, (STEPS + 1) * width), BF16),
            pltpu.VMEM((width, (STEPS + 1) * width), F32),
            pltpu.VMEM((width, (STEPS + 1) * width), F32),
            dma((planes,)),
            dma((depth,)),
            dma((LEADS,)),
            dma((LEADS, planes)),
            dma((LEADS,)),
            dma((LEADS,)),
            dma((LEADS,)),
            dma((REACH * DOWN,)),
            dma((REACH * DOWN,)),
            dma(((REACH + 1) * ups,)),
            dma(((REACH + 1) * ups,)),
            dma((STEPS + 2, 4)),
        ],
        compiler_params=pltpu.CompilerParams(
            collective_id=0, has_side_effects=True, vmem_limit_bytes=48 * 1024 * 1024
        ),
        cost_estimate=pl.CostEstimate(flops=20_000_000_000, bytes_accessed=6 * 1024 * 1024, transcendentals=0),
    )(local)
    return factor[:, :, None], second[:, None]


def solution(mesh, depth=DEPTH):
    n = mesh.shape["blk"]
    return jax.shard_map(
        functools.partial(body, n, depth),
        mesh=mesh,
        in_specs=(P(None, "blk", None, "ch"),),
        out_specs=(P(None, None, "blk", None, "ch"), P(None, "blk", None, "ch")),
        check_vma=False,
    )
```

time: 1140 us -> 138 us (0.12)
  waiting for transfers between devices: 934 us -> 0 us
  Pallas kernels: 0 us -> 130 us
  matrix products: 110 us -> 0 us
  blocking collectives: 25.4 us -> 0 us
  between operations: 22.4 us -> 0.65 us
  starting transfers between devices: 20.4 us -> 0 us
  other arithmetic: 15.4 us -> 0 us
    psum x4 -> x0, waiting for transfers between devices: 861 us -> none  [broadcast(): return lax.psum(block, axis)]
    pallas_call x0 -> x1, Pallas kernels: none -> 130 us  [body(): pl.pallas_call(functools.partial(kernel, n, depth), out_shape=(jax.ShapeD...]
    dot_general x156 -> x0, matrix products: 110 us -> none  [the longest x152 94.5 us: matmul(): return jnp.dot(left, right, precision=lax.Precision.HIGHEST)]
    ppermute x4 -> x0, waiting for transfers between devices: 73.4 us -> none  [passed_along(): lax.ppermute(array, axis, [(i, (i + by) % peers) for i in range(peers)])]
    all_gather x4 -> x0, blocking collectives: 25.4 us -> none  [the longest x3 18.4 us: body(): pair_whole = lax.all_gather(pair_half, 'ch', axis=2, tiled=True)]
    ppermute x4 -> x0, starting transfers between devices: 20.3 us -> none  [passed_along(): lax.ppermute(array, axis, [(i, (i + by) % peers) for i in range(peers)])]
  transfers between devices with their start and end apart: 8 -> 0, of which waited for: 8 -> 0; matrix products, arithmetic and copies ran while one was open for 0% -> 0% of each run, Pallas kernels for 0% -> 0%
where the time goes in v1:
time: 138 us
  Pallas kernels  130 us (94%)
  local copies, waits for them, and re-layouts  6.84 us (5%)
    pallas_call x1, Pallas kernels, body(): pl.pallas_call(functools.partial(kernel, n, depth), out_shape=(jax.ShapeD...  130 us
    unnamed x4, local copies, waits for them, and re-layouts  6.84 us

profile of v1, /device:TPU:1, one launch (start us, length us, event | category | flops | bytes accessed | tf_op | source)
XLA Modules:
  0.0 137.7 jit_solution(6009384055337867555)
XLA Ops:
  0.6 0.0 copy-start
  0.6 1.2 copy-done
  1.9 130.2 %shard_map.30 = (f32[4,8,256,128]{3,2,1,0:T(8,128)}, f32[8,256,128]{2,1,0:T(8,128)S(1)}) custom-call(f32[8,256,128]{2,1,0:T(8,128)S(1)} %bitcast.8), custom_call_target="tpu_custom_call" | custom-call | flops 20000000000 | bytes 6291456 | tf_op jit(solution)/shard_map/pallas_call | solution.py:335
  132.1 4.7 %copy.7 = f32[4,8,1,256,128]{4,3,2,1,0:T(8,128)} copy(f32[4,8,1,256,128]{4,3,2,1,0:T(8,128)} %bitcast.9) | data formatting | bytes 8388608
  136.7 1.0 copy.8
Async XLA Ops:
  0.6 1.2 copy-start

commit v2 on v1

--- a/solution.py
+++ b/solution.py
@@ -11,11 +11,17 @@
 F32, BF16 = jnp.float32, jnp.bfloat16
 
 STEPS = 3
+OWN_AT = (([0, 1, 2], [0]), ([3, 4], [1, 2]), ([], []), ([], []))
+AT_START = (([], []), ([10], [4]), ([13], [7]))
+AFTER_INVERSE = (([8], [2]), ([11], [5]), ([14], [8]))
+AFTER_ROOTS = (([9], [3]), ([12], [6]), ([], [9]))
 LEADS = STEPS + 1
 REACH = STEPS + 1
 DEPTH = 8
+SIDE = 4
 DOWN = 5
-FAR = 5
+FAR = REACH + 1
+RISE = 3
 
 
 def split(a):
@@ -40,9 +46,9 @@
     pltpu.make_async_copy(ref, ref, sem).wait()
 
 
-def kernel(n, depth, x_ref, factor_ref, second_ref, halo, lead, why, zed, stage, coef_high, coef_low, a_ref, c_ref,
-           scatter_send, z_send, piece_recv, plane_send, plane_recv, sib_send, sib_recv,
-           down_send, down_recv, up_send, up_recv, out_sem):
+def kernel(n, depth, side, x_ref, factor_ref, second_ref, halo, lead, why, zed, coef_high, coef_low, a_ref, c_ref,
+           scatter_send, z_send, piece_recv, y_send, y_recv, row_send, row_recv, sib_send, sib_recv,
+           down_send, down_recv, up_send, up_recv):
     width = x_ref.shape[1]
     count = x_ref.shape[0]
     half = x_ref.shape[2]
@@ -51,10 +57,21 @@
     planes = n // depth
     rows = width // planes
     p, z = lax.div(b, depth), lax.rem(b, depth)
-    below, above, far_below = lax.rem(b + n - 1, n), lax.rem(b + 1, n), lax.rem(b + n - FAR, n)
-
-    def in_plane(i):
-        return {"blk": lax.rem(p + i, planes) * depth + z}
+    below, above = lax.rem(b + n - 1, n), lax.rem(b + 1, n)
+    first_stop = p * depth + lax.rem(z + RISE, depth)
+    held_from = p * depth + lax.rem(z + depth - RISE, depth)
+    second_stop = lax.rem(held_from + n - REACH, n)
+    sender = lax.rem(b + REACH, n)
+    second_sender = lax.div(sender, depth) * depth + lax.rem(lax.rem(sender, depth) + RISE, depth)
+
+    across = planes // side
+    row, column = lax.div(p, side), lax.rem(p, side)
+
+    def in_row(i):
+        return {"blk": (row * side + lax.rem(column + i, side)) * depth + z}
+
+    def in_column(i):
+        return {"blk": (lax.rem(row + i, across) * side + column) * depth + z}
 
     def in_line(i):
         return {"blk": p * depth + lax.rem(z + i, depth)}
@@ -78,12 +95,27 @@
     def greet(to):
         pl.semaphore_signal(barrier, inc=1, device_id=to, device_id_type=MESH)
 
-    for by in (1, n - 1, FAR, n - FAR):
-        greet({"blk": lax.rem(b + by, n)})
+    for to in (above, below, held_from, second_sender):
+        greet({"blk": to})
     greet(sibling)
-    each(1, planes, lambda i: greet(in_plane(i)))
-    each(1, depth, lambda i: greet(in_line(i)))
-    pl.semaphore_wait(barrier, 4 + 1 + (planes - 1) + (depth - 1))
+    for i in range(1, side):
+        greet(in_row(i))
+    for i in range(1, across):
+        greet(in_column(i))
+    for item in range(LEADS):
+
+        @pl.when(z != item)
+        def _():
+            greet({"blk": p * depth + item})
+
+    @pl.when((z < LEADS) & (p > 0))
+    def _():
+        greet({"blk": z})
+
+    owner, forwards = (b < LEADS).astype(jnp.int32), (z < LEADS).astype(jnp.int32)
+    pl.semaphore_wait(
+        barrier, 5 + (side - 1) + (across - 1) + forwards * (depth - 1) + owner * (planes - 1)
+    )
 
     def piece(item, i):
         return lead.at[item, ch, pl.ds(pl.multiple_of(i * rows, rows), rows)]
@@ -97,11 +129,55 @@
     def line_copy(item, i):
         return push(piece(item, p), piece(item, p), z_send.at[i], piece_recv.at[item], in_line(i))
 
-    def plane_copy(item, i):
-        return push(piece(item, p), piece(item, p), plane_send.at[item, i], plane_recv.at[item], in_plane(i))
-
-    def sibling_copy(item):
-        return push(lead.at[item, ch], lead.at[item, ch], sib_send.at[item], sib_recv.at[item], sibling)
+    groups = ((0, 1), (1, LEADS - 1))
+
+    def lead_rows(g, start, size):
+        return lead.at[pl.ds(*groups[g]), ch, pl.ds(start, size)]
+
+    def ring(g, size, place, region, neighbour, sends, recvs):
+        def copy(k, part, by):
+            return push(region(g, part), region(g, part), sends.at[g, k], recvs.at[g, k], neighbour(by))
+
+        before, after = lax.rem(place + size - 1, size), lax.rem(place + 1, size)
+        copies = [copy(0, place, 1), copy(1, place, size - 1), copy(2, before, 1)][: size - 1]
+
+        def first():
+            for c in copies[:2]:
+                c.start()
+
+        def second():
+            if size > 1:
+                wait_for(region(g, before), recvs.at[g, 0])
+            if size > 3:
+                copies[2].start()
+
+        def third():
+            if size > 2:
+                wait_for(region(g, after), recvs.at[g, 1])
+            if size > 3:
+                wait_for(region(g, lax.rem(place + 2, size)), recvs.at[g, 2])
+
+        def sent():
+            for c in copies:
+                c.wait_send()
+
+        return first, second, third, sent
+
+    def row_region(g, i):
+        return lead_rows(g, pl.multiple_of((row * side + i) * rows, rows), rows)
+
+    def column_region(g, i):
+        return lead_rows(g, pl.multiple_of(i * side * rows, side * rows), side * rows)
+
+    row_rings = [ring(g, side, column, row_region, in_row, y_send, y_recv) for g in range(2)]
+    column_rings = [ring(g, across, row, column_region, in_column, row_send, row_recv) for g in range(2)]
+
+    def sibling_copy(g):
+        part = lead.at[pl.ds(*groups[g]), ch]
+        return push(part, part, sib_send.at[g], sib_recv.at[g], sibling)
+
+    def complete(g):
+        wait_for(lead.at[pl.ds(*groups[g]), 1 - ch], sib_recv.at[g])
 
     @pl.when(b < LEADS)
     def _():
@@ -130,39 +206,56 @@
     def up_arrived(t):
         wait_for(halo.at[FAR - 1 - lax.div(t, ups), DOWN + lax.rem(t, ups)], up_recv.at[t])
 
-    def relay(t):
-        @pl.when(t < n_down - DOWN)
-        def _():
+    def relay(downs=(), upwards=()):
+        for t in downs:
             down_arrived(t)
             down_copy(t + DOWN, down_source(t + DOWN)).start()
-
-        @pl.when(t < n_up - ups)
-        def _():
+        for t in upwards:
             up_arrived(t)
-            up_copy(t + ups, up_source(t + ups), above).start()
-
-    each(0, ups, lambda t: up_copy(t, x_ref.at[DOWN + t], far_below).start())
-    each(0, 1, lambda t: down_copy(t, x_ref.at[t]).start())
-
-    def pass_piece(item):
-        wait_for(piece(item, p), piece_recv.at[item])
-
-        @pl.when(z == item)
-        def _():
-            each(1, depth, lambda i: line_copy(item, i).start())
-
-        each(1, planes, lambda i: plane_copy(item, i).start())
-
-    each(0, LEADS, pass_piece)
-    each(1, DOWN, lambda t: down_copy(t, x_ref.at[t]).start())
-
-    def gathered(item):
-        if planes > 1:
-            wait_for(lead.at[item, ch, pl.ds(0, (planes - 1) * rows)], plane_recv.at[item])
-        sibling_copy(item).start()
-
-    def complete(item):
-        wait_for(lead.at[item, 1 - ch], sib_recv.at[item])
+            up_copy(t + ups, up_source(t + ups), second_stop if t < ups else above).start()
+
+    def own(downs=(), upwards=()):
+        for t in downs:
+            down_copy(t, x_ref.at[t]).start()
+        for t in upwards:
+            up_copy(t, x_ref.at[DOWN + t], first_stop).start()
+
+    def pass_pieces(g):
+        first, size = groups[g]
+        for item in range(first, first + size):
+
+            @pl.when(z != item)
+            def _():
+                wait_for(piece(item, p), piece_recv.at[item])
+
+        row_rings[g][0]()
+
+    own(*OWN_AT[0])
+
+    @pl.when(z < LEADS)
+    def _():
+        wait_for(piece(z, p), piece_recv.at[z])
+        each(1, depth, lambda i: line_copy(z, i).start())
+
+    own(*OWN_AT[1])
+    pass_pieces(0)
+    pass_pieces(1)
+    own(*OWN_AT[2])
+    row_rings[0][1]()
+    row_rings[1][1]()
+    for g in range(2):
+        row_rings[g][2]()
+        column_rings[g][0]()
+    own(*OWN_AT[3])
+    column_rings[0][1]()
+    column_rings[1][1]()
+    relay([0, 1])
+    column_rings[0][2]()
+    sibling_copy(0).start()
+    relay([2])
+    column_rings[1][2]()
+    sibling_copy(1).start()
+    relay([3])
 
     def lead_block(item):
         return jnp.concatenate([lead[item, 0], lead[item, 1]], axis=1)
@@ -174,7 +267,7 @@
     def scale_of(a):
         return jnp.max(jnp.sum(jnp.abs(a), axis=0, keepdims=True), axis=1, keepdims=True)
 
-    def roots(matrices, sweeps, first_tick):
+    def roots(matrices, sweeps):
         kept = range(len(matrices))
         scales = [scale_of(a) for a in matrices]
         starts = [a * (1.0 / s) for a, s in zip(matrices, scales)]
@@ -185,7 +278,6 @@
             why[i] = firsts[i]
 
         def sweep(k, carry):
-            relay(first_tick + k)
             ys = [split(why[i]) for i in kept]
             zs = [split(zed[i]) for i in kept]
             ts = [split(1.5 * eye - 0.5 * dot_of_parts(zs[i], ys[i])) for i in kept]
@@ -207,27 +299,26 @@
         coef_high[o, :, : terms * width] = high
         coef_low[o, :, : terms * width] = low
 
-    gathered(0)
     complete(0)
-    (s,) = roots([lead_block(0)], 6, 0)
+    relay([4])
+    (s,) = roots([lead_block(0)], 6)
+    relay([5, 6], [0])
     root = jnp.sqrt(s)
     w = zed[0] * (1.0 / root)
     x0 = why[0] * root
-    for item in range(1, LEADS):
-        gathered(item)
-    for item in range(1, LEADS):
-        complete(item)
+    complete(1)
     rest = mul(w, jnp.concatenate([lead_block(item) for item in range(1, LEADS)], axis=1))
     uppers = [x0] + [rest[:, i * width : (i + 1) * width] for i in range(LEADS - 1)]
     lowers = uppers[1:]
     keep_coefficients(0, w, 1)
     a_ref[:, cols(0)] = w
     c_ref[:, cols(0)] = w
-    tick = 5
+    relay([7], [1])
 
     for k in range(STEPS):
         terms = k + 1
         x, y = uppers[0], lowers[0]
+        relay(*AT_START[k])
         both = mul(x, jnp.concatenate([x.T, y.T], axis=1))
         gram, cross = both[:, :width], both[:, width:]
         s = 1.0 / scale_of(gram)
@@ -239,8 +330,9 @@
         kt = total + mul(power, total)
         kk = kt.T
         kt_parts, kk_parts = split(kt), split(kk)
-        scales = roots([eye - dot_of_parts(kt_parts, kk_parts), eye - dot_of_parts(kk_parts, kt_parts)], 5, tick)
-        tick += 4
+        relay(*AFTER_INVERSE[k])
+        scales = roots([eye - dot_of_parts(kt_parts, kk_parts), eye - dot_of_parts(kk_parts, kt_parts)], 5)
+        relay(*AFTER_ROOTS[k])
         first = zed[0] * (1.0 / jnp.sqrt(scales[0]))
         second = zed[1] * (1.0 / jnp.sqrt(scales[1]))
         first_parts, second_parts = split(first), split(second)
@@ -280,32 +372,56 @@
                 blocks.append(jnp.where(r + wrapped < count, block, jnp.zeros_like(block)))
         return split(jnp.concatenate(blocks, axis=1))
 
-    def out_copy(o, q):
-        target = factor_ref.at[o, pl.ds(2 * q, 2)] if o <= STEPS else second_ref.at[pl.ds(2 * q, 2)]
-        return pltpu.make_async_copy(stage.at[o, pl.ds(2 * q, 2)], target, out_sem.at[o, q])
-
-    def emit(o, q, parts):
-        terms = len(parts)
-        high, low = coef_high[o, :, : terms * width], coef_low[o, :, : terms * width]
-        rh = jnp.concatenate([part[0] for part in parts], axis=0)
-        rl = jnp.concatenate([part[1] for part in parts], axis=0)
-        value = dot_of_parts((high, low), (rh, rl))
-        stage[o, 2 * q] = value[:, :half]
-        stage[o, 2 * q + 1] = value[:, half:]
-        out_copy(o, q).start()
-
-    def emit_pair(q, outputs):
-        last = REACH if STEPS + 1 in outputs else max(outputs)
-        parts = [data(j, q) for j in range(last + 1)]
-        for o in outputs:
-            emit(o, q, parts[: o + 1] if o <= STEPS else parts[1:])
-
-    each(0, 4, lambda q: emit_pair(q, [0]))
-    each(0, 2, lambda q: emit_pair(q, [1, 2, 3]))
+    def terms_of(o, q, slots, add):
+        shift = 1 if o > STEPS else 0
+        parts = [data(j, q) for j in slots]
+        left = [
+            jnp.concatenate([ref[o, :, (j - shift) * width : (j - shift + 1) * width] for j in slots], axis=1)
+            for ref in (coef_high, coef_low)
+        ]
+        right = [jnp.concatenate([part[i] for part in parts], axis=0) for i in range(2)]
+        value = dot_of_parts(left, right)
+        for i in range(2):
+            cut = value[:, i * half : (i + 1) * half]
+            r = 2 * q + i
+            if o > STEPS:
+                second_ref[r] = second_ref[r] + cut if add else cut
+            else:
+                factor_ref[o, r] = factor_ref[o, r] + cut if add else cut
+
+    def own_row(q):
+        terms_of(0, q, [0], False)
+
+    def near_rows(q):
+        for o in range(1, STEPS + 1):
+            terms_of(o, q, list(range(o + 1)), False)
+        terms_of(STEPS + 1, q, [1, 2, 3], False)
+
+    def near_last(q):
+        terms_of(STEPS + 1, q, [4], True)
+
+    def far_rows(q, row):
+        terms_of(2, q, [0, 2], False)
+        terms_of(3, q, [0, 2, 3], False)
+        terms_of(4, q, row, False)
+
+    def far_last(q, row):
+        terms_of(1, q, [0, 1], False)
+        for o in range(2, STEPS + 1):
+            terms_of(o, q, [1], True)
+        terms_of(STEPS + 1, q, row, True)
+
+    relay([], [10])
+    each(0, 4, own_row)
+    relay([], [11])
+    each(0, 2, near_rows)
+    far_rows(2, [2, 3])
+    far_rows(3, [2, 3, 4])
     each(n_down - DOWN, n_down, down_arrived)
-    each(0, 2, lambda q: emit_pair(q, [4]))
+    each(0, 2, near_last)
     each(n_up - ups, n_up, up_arrived)
-    each(2, 4, lambda q: emit_pair(q, [1, 2, 3, 4]))
+    far_last(2, [1, 4])
+    far_last(3, [1])
 
     @pl.when(b < LEADS)
     def _():
@@ -316,36 +432,34 @@
     def _():
         each(1, depth, lambda i: line_copy(z, i).wait_send())
 
-    for item in range(LEADS):
-        each(1, planes, lambda i: plane_copy(item, i).wait_send())
-        sibling_copy(item).wait_send()
+    for g in range(len(groups)):
+        row_rings[g][3]()
+        column_rings[g][3]()
+        sibling_copy(g).wait_send()
     each(0, n_down, lambda t: down_copy(t, x_ref.at[0]).wait_send())
     each(0, n_up, lambda t: up_copy(t, x_ref.at[0], above).wait_send())
-    for o in range(STEPS + 2):
-        each(0, 4, lambda q: out_copy(o, q).wait())
-
-
-def body(n, depth, blocks):
+
+
+def body(n, depth, side, blocks):
     local = blocks[:, 0]
     count, width, half = local.shape
     ups = count - DOWN
     planes = n // depth
     dma = pltpu.SemaphoreType.DMA
-    any_space = pl.BlockSpec(memory_space=pl.ANY)
+    in_vmem = pl.BlockSpec(memory_space=pltpu.VMEM)
     factor, second = pl.pallas_call(
-        functools.partial(kernel, n, depth),
+        functools.partial(kernel, n, depth, side),
         out_shape=(
             jax.ShapeDtypeStruct((STEPS + 1, count, width, half), F32),
             jax.ShapeDtypeStruct((count, width, half), F32),
         ),
-        in_specs=[pl.BlockSpec(memory_space=pltpu.VMEM)],
-        out_specs=(any_space, any_space),
+        in_specs=[in_vmem],
+        out_specs=(in_vmem, in_vmem),
         scratch_shapes=[
             pltpu.VMEM((FAR, count, width, half), F32),
             pltpu.VMEM((LEADS, 2, width, half), F32),
             pltpu.VMEM((2, width, width), F32),
             pltpu.VMEM((2, width, width), F32),
-            pltpu.VMEM((STEPS + 2, count, width, half), F32),
             pltpu.VMEM((STEPS + 2, width, (STEPS + 1) * width), BF16),
             pltpu.VMEM((STEPS + 2, width, (STEPS + 1) * width), BF16),
             pltpu.VMEM((width, (STEPS + 1) * width), F32),
@@ -353,28 +467,29 @@
             dma((planes,)),
             dma((depth,)),
             dma((LEADS,)),
-            dma((LEADS, planes)),
-            dma((LEADS,)),
-            dma((LEADS,)),
-            dma((LEADS,)),
+            dma((2, 3)),
+            dma((2, 3)),
+            dma((2, 3)),
+            dma((2, 3)),
+            dma((2,)),
+            dma((2,)),
             dma((REACH * DOWN,)),
             dma((REACH * DOWN,)),
             dma(((REACH + 1) * ups,)),
             dma(((REACH + 1) * ups,)),
-            dma((STEPS + 2, 4)),
         ],
         compiler_params=pltpu.CompilerParams(
-            collective_id=0, has_side_effects=True, vmem_limit_bytes=48 * 1024 * 1024
+            collective_id=0, has_side_effects=True, vmem_limit_bytes=40 * 1024 * 1024
         ),
         cost_estimate=pl.CostEstimate(flops=20_000_000_000, bytes_accessed=6 * 1024 * 1024, transcendentals=0),
     )(local)
     return factor[:, :, None], second[:, None]
 
 
-def solution(mesh, depth=DEPTH):
+def solution(mesh, depth=DEPTH, side=SIDE):
     n = mesh.shape["blk"]
     return jax.shard_map(
-        functools.partial(body, n, depth),
+        functools.partial(body, n, depth, side),
         mesh=mesh,
         in_specs=(P(None, "blk", None, "ch"),),
         out_specs=(P(None, None, "blk", None, "ch"), P(None, "blk", None, "ch")),

time: 138 us -> 116 us (0.84)
  the two profiles are of different devices: /device:TPU:1 before, /device:TPU:12 now
where the time goes in v2:
time: 116 us
  Pallas kernels  111 us (96%)
  local copies, waits for them, and re-layouts  4.2 us (4%)
    pallas_call x1, Pallas kernels, body(): pl.pallas_call(functools.partial(kernel, n, depth, side), out_shape=(jax....  111 us
    unnamed x4, local copies, waits for them, and re-layouts  4.2 us

profile of v2, /device:TPU:12, one launch (start us, length us, event | category | flops | bytes accessed | tf_op | source)
XLA Modules:
  0.0 115.7 jit_solution(5981346461496764976)
XLA Ops:
  0.6 0.0 copy-start
  0.6 1.2 %copy-done = f32[8,1,256,128]{3,2,1,0:T(8,128)S(1)} copy-done((f32[8,1,256,128]{3,2,1,0:T(8,128)S(1)}, f32[8,1,256,128]{3,2,1,0:T(8,128)}, u32[]{:S(2)}) %copy-start) | copy-done | bytes 1048600
  1.9 110.9 %shard_map.30 = (f32[4,8,256,128]{3,2,1,0:T(8,128)S(1)}, f32[8,256,128]{2,1,0:T(8,128)S(1)}) custom-call(f32[8,256,128]{2,1,0:T(8,128)S(1)} %bitcast.9), custom_call_target="tpu_custom_call" | custom-call | flops 20000000000 | bytes 6291456 | tf_op jit(solution)/shard_map/pallas_call | solution.py:450
  112.7 2.0 %copy.7 = f32[4,8,1,256,128]{4,3,2,1,0:T(8,128)} copy(f32[4,8,1,256,128]{4,3,2,1,0:T(8,128)S(1)} %bitcast.7) | data formatting | bytes 8388608
  114.8 1.0 copy.8
Async XLA Ops:
  0.6 1.2 %copy-start = (f32[8,1,256,128]{3,2,1,0:T(8,128)S(1)}, f32[8,1,256,128]{3,2,1,0:T(8,128)}, u32[]{:S(2)}) copy-start(f32[8,1,256,128]{3,2,1,0:T(8,128)} %param.1) | copy-start | bytes 3145732

commit v3 on v2

--- a/solution.py
+++ b/solution.py
@@ -138,24 +138,25 @@
         def copy(k, part, by):
             return push(region(g, part), region(g, part), sends.at[g, k], recvs.at[g, k], neighbour(by))
 
-        before, after = lax.rem(place + size - 1, size), lax.rem(place + 1, size)
-        copies = [copy(0, place, 1), copy(1, place, size - 1), copy(2, before, 1)][: size - 1]
+        behind = [lax.rem(place + size - i, size) for i in range(size)]
+        copies = [copy(i, behind[i], 1) for i in range(size - 1)]
 
         def first():
-            for c in copies[:2]:
+            for c in copies[:1]:
+                c.start()
+
+        def arrived(i):
+            wait_for(region(g, behind[i]), recvs.at[g, i - 1])
+            for c in copies[i : i + 1]:
                 c.start()
 
         def second():
             if size > 1:
-                wait_for(region(g, before), recvs.at[g, 0])
-            if size > 3:
-                copies[2].start()
+                arrived(1)
 
         def third():
-            if size > 2:
-                wait_for(region(g, after), recvs.at[g, 1])
-            if size > 3:
-                wait_for(region(g, lax.rem(place + 2, size)), recvs.at[g, 2])
+            for i in range(2, size):
+                arrived(i)
 
         def sent():
             for c in copies:

time: 116 us -> 104 us (0.90)
  the two profiles are of different devices: /device:TPU:12 before, /device:TPU:1 now
where the time goes in v3:
time: 104 us
  Pallas kernels  99.5 us (96%)
  local copies, waits for them, and re-layouts  4.2 us (4%)
    pallas_call x1, Pallas kernels, body(): pl.pallas_call(functools.partial(kernel, n, depth, side), out_shape=(jax....  99.5 us
    unnamed x4, local copies, waits for them, and re-layouts  4.2 us

profile of v3, /device:TPU:1, one launch (start us, length us, event | category | flops | bytes accessed | tf_op | source)
XLA Modules:
  0.0 104.4 jit_solution(1724615984486728330)
XLA Ops:
  0.6 0.0 copy-start
  0.6 1.2 %copy-done = f32[8,1,256,128]{3,2,1,0:T(8,128)S(1)} copy-done((f32[8,1,256,128]{3,2,1,0:T(8,128)S(1)}, f32[8,1,256,128]{3,2,1,0:T(8,128)}, u32[]{:S(2)}) %copy-start) | copy-done | bytes 1048600
  1.9 99.5 %shard_map.30 = (f32[4,8,256,128]{3,2,1,0:T(8,128)S(1)}, f32[8,256,128]{2,1,0:T(8,128)S(1)}) custom-call(f32[8,256,128]{2,1,0:T(8,128)S(1)} %bitcast.9), custom_call_target="tpu_custom_call" | custom-call | flops 20000000000 | bytes 6291456 | tf_op jit(solution)/shard_map/pallas_call | solution.py:451
  101.4 2.0 %copy.7 = f32[4,8,1,256,128]{4,3,2,1,0:T(8,128)} copy(f32[4,8,1,256,128]{4,3,2,1,0:T(8,128)S(1)} %bitcast.7) | data formatting | bytes 8388608
  103.4 1.0 copy.8
Async XLA Ops:
  0.6 1.2 %copy-start = (f32[8,1,256,128]{3,2,1,0:T(8,128)S(1)}, f32[8,1,256,128]{3,2,1,0:T(8,128)}, u32[]{:S(2)}) copy-start(f32[8,1,256,128]{3,2,1,0:T(8,128)} %param.1) | copy-start | bytes 3145732

commit v4 on v3

--- a/solution.py
+++ b/solution.py
@@ -11,7 +11,7 @@
 F32, BF16 = jnp.float32, jnp.bfloat16
 
 STEPS = 3
-OWN_AT = (([0, 1, 2], [0]), ([3, 4], [1, 2]), ([], []), ([], []))
+OWN_AT = (([0, 1], []), ([2, 3, 4], [0, 1, 2]), ([], []), ([], []))
 AT_START = (([], []), ([10], [4]), ([13], [7]))
 AFTER_INVERSE = (([8], [2]), ([11], [5]), ([14], [8]))
 AFTER_ROOTS = (([9], [3]), ([12], [6]), ([], [9]))

time: 104 us -> 103 us (level)
  Pallas kernels: 99.5 us -> 98.1 us
    pallas_call x1, Pallas kernels: 99.5 us -> 98.1 us  [body(): pl.pallas_call(functools.partial(kernel, n, depth, side), out_shape=(jax....]
where the time goes in v4:
time: 103 us
  Pallas kernels  98.1 us (95%)
  local copies, waits for them, and re-layouts  4.2 us (4%)
    pallas_call x1, Pallas kernels, body(): pl.pallas_call(functools.partial(kernel, n, depth, side), out_shape=(jax....  98.1 us
    unnamed x4, local copies, waits for them, and re-layouts  4.2 us

profile of v4, /device:TPU:1, one launch (start us, length us, event | category | flops | bytes accessed | tf_op | source)
XLA Modules:
  0.0 102.9 jit_solution(1455546764136935700)
XLA Ops:
  0.6 0.0 copy-start
  0.6 1.2 %copy-done = f32[8,1,256,128]{3,2,1,0:T(8,128)S(1)} copy-done((f32[8,1,256,128]{3,2,1,0:T(8,128)S(1)}, f32[8,1,256,128]{3,2,1,0:T(8,128)}, u32[]{:S(2)}) %copy-start) | copy-done | bytes 1048600
  1.9 98.1 %shard_map.30 = (f32[4,8,256,128]{3,2,1,0:T(8,128)S(1)}, f32[8,256,128]{2,1,0:T(8,128)S(1)}) custom-call(f32[8,256,128]{2,1,0:T(8,128)S(1)} %bitcast.9), custom_call_target="tpu_custom_call" | custom-call | flops 20000000000 | bytes 6291456 | tf_op jit(solution)/shard_map/pallas_call | solution.py:451
  100.0 2.0 %copy.7 = f32[4,8,1,256,128]{4,3,2,1,0:T(8,128)} copy(f32[4,8,1,256,128]{4,3,2,1,0:T(8,128)S(1)} %bitcast.7) | data formatting | bytes 8388608
  102.0 1.0 copy.8
Async XLA Ops:
  0.6 1.2 %copy-start = (f32[8,1,256,128]{3,2,1,0:T(8,128)S(1)}, f32[8,1,256,128]{3,2,1,0:T(8,128)}, u32[]{:S(2)}) copy-start(f32[8,1,256,128]{3,2,1,0:T(8,128)} %param.1) | copy-start | bytes 3145732
